TPU v7x, 512 devices: a whole 4x8x8 slice. The times are simulated.
512 devices in a mesh: feat: 8 (over z), vocab: 64 (over x, y, core).
Axes of the slice: x: 4, y: 8, z: 8, core: 2. Of those that a mesh axis runs over, the one named last changes fastest.
Arguments:
- hidden: bfloat16 [4, 512, 7168], P(None, 'feat', 'vocab'), may hold values from -6 to 6
- down_factor: bfloat16 [7168, 1024], P('vocab', 'feat'), may hold values from -0.0625 to 0.0625
- unembed: bfloat16 [131072, 1024], P('vocab'), may hold values from -5 to 5
- targets: int32 [4, 512], P(None, 'feat'), may hold values from 0 to 131071
- depth_scale: float32 [4], replicated, may hold values from 16 to 128
Outputs:
- row_loss: float32 [4, 512], P(None, 'feat')
- grad_hidden: float32 [4, 512, 7168], P(None, 'feat', 'vocab')
- grad_down: float32 [7168, 1024], P('vocab', 'feat')
- grad_unembed: bfloat16 [131072, 1024], P('vocab', 'feat')
All inputs are finite; a program needn't handle non-finite values.
Results may differ from a plain program's by a relative error of at most 0.012.
The roundings to bfloat16 on the way count: a program that leaves them out, or rounds other values in their place, can miss the bound.
Values may be sent and summed in bfloat16 or wider, within the bound.
A program may use at most 64 MiB of HBM per device.

v0:
```python
import jax
import jax.numpy as jnp
from jax import lax
from jax.sharding import PartitionSpec as P


def shards(hidden, down_factor, unembed, targets, depth_scale):
    full_down = lax.all_gather(down_factor, "feat", axis=1, tiled=True)
    partial_value = jnp.einsum("krd,dc->krc", hidden, full_down, preferred_element_type=jnp.float32)
    codes = lax.psum(partial_value, "vocab").astype(jnp.bfloat16)
    logits = jnp.einsum("krc,vc->krv", codes, unembed, preferred_element_type=jnp.float32)
    voc_dev = unembed.shape[0]
    offset = lax.axis_index("vocab") * voc_dev
    columns = offset + jnp.arange(voc_dev, dtype=jnp.int32)
    hits = targets[:, :, None] == columns[None, None, :]
    local_peak = jnp.max(logits, axis=-1)
    target_part = jnp.sum(jnp.where(hits, logits, 0.0), axis=-1)
    peak = lax.pmax(local_peak, "vocab")
    local_total = jnp.sum(jnp.exp(logits - peak[:, :, None]), axis=-1)
    total, picked = lax.psum((local_total, target_part), "vocab")
    row_loss = peak + jnp.log(total) - picked
    probs = jnp.exp(logits - peak[:, :, None]) / total[:, :, None]
    grad_logits = (depth_scale[:, None, None] * (probs - hits.astype(jnp.float32))).astype(
        jnp.bfloat16
    )
    code_terms = jnp.einsum("krv,vc->krc", grad_logits, unembed, preferred_element_type=jnp.float32)
    grad_codes = lax.psum(code_terms, "vocab").astype(jnp.bfloat16)
    grad_hidden = jnp.einsum(
        "krc,dc->krd", grad_codes, full_down, preferred_element_type=jnp.float32
    )
    code_cols, grad_cols = (
        lax.all_to_all(codes, "feat", split_axis=2, concat_axis=1, tiled=True),
        lax.all_to_all(grad_codes, "feat", split_axis=2, concat_axis=1, tiled=True),
    )
    block = grad_cols
    grad_down = jnp.einsum(
        "krd,krc->dc",
        lax.all_gather(hidden, "feat", axis=1, tiled=True),
        block,
        preferred_element_type=jnp.float32,
    )
    block = code_cols
    grad_unembed = jnp.einsum(
        "krv,krc->vc",
        lax.all_gather(grad_logits, "feat", axis=1, tiled=True),
        block,
        preferred_element_type=jnp.float32,
    ).astype(jnp.bfloat16)
    return (row_loss, grad_hidden, grad_down, grad_unembed)


def solution(mesh):
    placed = (P(None, "feat", "vocab"), P("vocab", "feat"), P("vocab", None), P(None, "feat"), P())
    return jax.shard_map(
        shards,
        mesh=mesh,
        in_specs=placed,
        out_specs=(
            P(None, "feat"),
            P(None, "feat", "vocab"),
            P("vocab", "feat"),
            P("vocab", "feat"),
        ),
        check_vma=False,
    )
```

profile of v0, /device:TPU:1, one launch (start us, length us, event | category | flops | bytes accessed | tf_op | source)
XLA Modules:
  0.0 871.2 jit_solution(14494776319498910079)
XLA Ops:
  7.2 0.0 all-gather.2.cloned.1.call-start
  7.2 24.5 %all_gather.9 = bf16[112,1024]{1,0:T(8,128)(2,1)S(1)} all-gather(bf16[112,128]{1,0:T(8,128)(2,1)} %param.6), channel_id=1, replica_groups=mesh['feat'=8,'vocab'=64] {'feat'}, dimensions={1}, use_global_device_ids=true | all-gather | bytes 258048 | tf_op jit(solution)/shard_map/all_gather | solution.py:8
  31.8 1.1 fusion.12
  32.9 255.1 %all-reduce.3 = bf16[4,64,1024]{2,1,0:T(8,128)(2,1)S(1)} all-reduce(f32[4,64,1024]{2,1,0:T(8,128)S(1)} %fusion.12), channel_id=1, replica_groups=mesh['feat'=8,'vocab'=64] {'vocab'}, use_global_device_ids=true, to_apply=%region_0.0 | all-reduce | flops 262144 | bytes 1572864 | tf_op jit(solution)/shard_map/psum | solution.py:10
  288.0 0.0 copy-start.1
  288.0 3.6 fusion.14
  291.5 0.0 copy-start.2
  291.5 129.1 %pmax.7 = f32[4,64]{1,0:T(4,128)S(1)} all-reduce(f32[4,64]{1,0:T(4,128)S(1)} %get-tuple-element.8), channel_id=1, replica_groups=mesh['feat'=8,'vocab'=64] {'vocab'}, use_global_device_ids=true, to_apply=%region_2.3 | all-reduce | flops 256 | bytes 2048 | tf_op jit(solution)/shard_map/pmax | solution.py:18
  420.7 0.0 copy-done.1
  420.7 0.6 fusion.9
  421.3 124.0 %psum.29 = f32[4,64]{1,0:T(4,128)S(1)} all-reduce(f32[4,64]{1,0:T(4,128)S(1)} %get-tuple-element.4), channel_id=1, replica_groups=mesh['feat'=8,'vocab'=64] {'vocab'}, use_global_device_ids=true, to_apply=%region_4.5 | all-reduce | flops 256 | bytes 2048 | tf_op jit(solution)/shard_map/psum | solution.py:20
  545.3 0.0 copy-done.2
  545.3 1.8 fusion.8
  547.1 0.0 all-gather.2.cloned.1.call-update
  547.1 3.8 fusion
  550.9 252.8 %all-reduce.4 = (f32[4,64]{1,0:T(4,128)S(1)}, bf16[4,64,1024]{2,1,0:T(8,128)(2,1)S(1)}) all-reduce(f32[4,64]{1,0:T(4,128)S(1)} %get-tuple-element.5, f32[4,64,1024]{2,1,0:T(8,128)S(1)} %fusion), channel_id=1, replica_groups=mesh['feat'=8,'vocab'=64] {'vocab'}, use_global_device_ids=true, to_apply=%region_6.7 | all-reduce | flops 262400 | bytes 1574912 | tf_op jit(solution)/shard_map/psum | solution.py:20
  803.7 0.7 copy.11
  804.4 1.5 reshape.20
  805.9 4.7 all-to-all-start
  810.6 0.0 copy-start
  810.6 0.7 copy.13
  811.3 1.5 reshape.22
  812.9 10.1 %all-to-all-done = bf16[8,2,16384]{2,1,0:T(2,128)(2,1)S(1)} async-done(((bf16[8,2,16384]{2,1,0:T(2,128)(2,1)}), bf16[8,2,16384]{2,1,0:T(2,128)(2,1)S(1)}, u32[]{:S(2)}, u32[]{:S(2)}) %all-to-all-start) | async-done | bytes 524320 | tf_op jit(solution)/shard_map/all_to_all | solution.py:33
  822.9 3.5 all-to-all-start.1
  826.4 0.0 copy-done
  826.4 26.1 %all_gather.10 = bf16[4,512,112]{2,1,0:T(8,128)(2,1)S(1)} all-gather(bf16[4,64,112]{2,1,0:T(8,128)(2,1)S(1)} %copy-done), channel_id=1, replica_groups=mesh['feat'=8,'vocab'=64] {'feat'}, dimensions={1}, use_global_device_ids=true | all-gather | bytes 516096 | tf_op jit(solution)/shard_map/all_gather | solution.py:38
  852.6 0.6 add_subtract_fusion
  853.2 1.0 fusion.10
  854.1 0.6 reshape.21
  854.8 0.7 copy.12
  855.5 0.0 all-to-all-done.1
  855.5 0.6 reshape.23
  856.1 0.7 copy.14
  856.9 1.0 convolution_bitcast_fusion.1
  857.8 0.0 all-gather.2.cloned.1.call-done
  857.8 6.6 fusion.4
  (1 shorter events, 0.0 us)
Async XLA Ops:
  7.2 850.7 %all-gather.2.cloned.1.call-start = ((), (), s32[]{:S(2)}) async-start(), calls=%async_computation.2 | async-start | bytes 9437184 | tf_op jit(solution)/shard_map/all_gather | solution.py:45
  288.0 132.7 %copy-start.1 = (s32[4,64]{1,0:T(4,128)S(1)}, s32[4,64]{1,0:T(4,128)}, u32[]{:S(2)}) copy-start(s32[4,64]{1,0:T(4,128)} %param.8) | copy-start | bytes 3076
  291.5 253.8 %copy-start.2 = (f32[4]{0:T(128)S(1)}, f32[4]{0:T(128)}, u32[]{:S(2)}) copy-start(f32[4]{0:T(128)} %param.9) | copy-start | bytes 52
  805.9 17.0 %all-to-all-start = ((bf16[8,2,16384]{2,1,0:T(2,128)(2,1)}), bf16[8,2,16384]{2,1,0:T(2,128)(2,1)S(1)}, u32[]{:S(2)}, u32[]{:S(2)}) async-start(bf16[8,2,16384]{2,1,0:T(2,128)(2,1)} %reshape.20), calls=%async_computation | async-start | bytes 1048576 | tf_op jit(solution)/shard_map/all_to_all | solution.py:33
  810.6 15.8 %copy-start = (bf16[4,64,112]{2,1,0:T(8,128)(2,1)S(1)}, bf16[4,64,112]{2,1,0:T(8,128)(2,1)}, u32[]{:S(2)}) copy-start(bf16[4,64,112]{2,1,0:T(8,128)(2,1)} %param.5) | copy-start | bytes 172036
  822.9 32.6 %all-to-all-start.1 = ((bf16[8,2,16384]{2,1,0:T(2,128)(2,1)}), bf16[8,2,16384]{2,1,0:T(2,128)(2,1)S(1)}, u32[]{:S(2)}, u32[]{:S(2)}) async-start(bf16[8,2,16384]{2,1,0:T(2,128)(2,1)} %reshape.22), calls=%async_computation.1 | async-start | bytes 1048576 | tf_op jit(solution)/shard_map/all_to_all | solution.py:32
Sparse Core Ops, SparseCore 0:
  547.3 89.1 all-gather.1
where the time goes:
time: 885 us; the launch traced here: 871 us
  blocking collectives  812 us (92%)
  matrix products  16.9 us (2%)
  between operations  14.2 us (2%)
  waiting for transfers between devices  10.1 us (1%)
    psum x2, blocking collectives, shards(): total, picked = lax.psum((local_total, target_part), 'vocab')  377 us
    psum x1, blocking collectives, shards(): codes = lax.psum(partial_value, 'vocab').astype(jnp.bfloat16)  255 us
    pmax x1, blocking collectives, shards(): peak = lax.pmax(local_peak, 'vocab')  129 us
    all_gather x1, blocking collectives, shards(): lax.all_gather(hidden, 'feat', axis=1, tiled=True)  26.1 us
    all_gather x1, blocking collectives, shards(): full_down = lax.all_gather(down_factor, 'feat', axis=1, tiled=True)  24.5 us
  transfers between devices with their start and end apart: 3, of which 1 were waited for; matrix products, arithmetic and copies ran while one was open for 2% of the time, Pallas kernels for 0%

commit v1 on v0

v1 whole, which is shorter than its diff:
```python
import functools

import jax
import jax.numpy as jnp
from jax import lax
from jax.experimental import pallas as pl
from jax.experimental.pallas import tpu as pltpu
from jax.sharding import PartitionSpec as P

MESH = pl.DeviceIdType.MESH
F32, BF16 = jnp.float32, jnp.bfloat16
TILE = 512
NT = (((1,), (1,)), ((), ()))
TN = (((0,), (0,)), ((), ()))


def far_first(n):
    return sorted(range(1, n), key=lambda d: -min(d, n - d))


class Kernel:
    def __init__(self, dims, rows, rank, width, vocab):
        self.X, self.Y, self.C, self.Z = dims
        self.rows, self.rank, self.width, self.vocab = rows, rank, width, vocab
        self.half = rows // self.C
        self.part = self.half // self.X
        self.col = rank // self.Y
        self.code_col = rank // self.Z
        self.sems = 0

    def scratch(self):
        X, Y, Z = self.X, self.Y, self.Z
        rows, rank, half, part, col = self.rows, self.rank, self.half, self.part, self.col

        def reduce_set():
            return [
                pltpu.VMEM((rows, rank), F32),
                pltpu.VMEM((half, rank), F32),
                pltpu.VMEM((half, rank), F32),
                pltpu.VMEM((X - 1 or 1, part, rank), F32),
                pltpu.VMEM((part, rank), F32),
                pltpu.VMEM((Y - 1 or 1, part, col), F32),
            ]

        return [
            pltpu.VMEM((self.vocab, rank), BF16),
            pltpu.VMEM((self.width, rank), BF16),
            pltpu.VMEM((Z, rows, self.width), BF16),
            pltpu.VMEM((Z, 8, rows), F32),
            *reduce_set(),
            *reduce_set(),
            pltpu.VMEM((Z, rows, rank), BF16),
            pltpu.VMEM((rows, rank), BF16),
            pltpu.VMEM((Z, rows, self.code_col), BF16),
            pltpu.VMEM((self.vocab, rows), F32),
            pltpu.VMEM((self.vocab, rows), BF16),
            pltpu.VMEM((rows, self.vocab), BF16),
            pltpu.VMEM((self.vocab, self.code_col), F32),
            pltpu.VMEM((3, 8, rows), F32),
            pltpu.VMEM((8, rows), F32),
            pltpu.VMEM((X - 1 or 1, 8, rows), F32),
            pltpu.VMEM((Y - 1 or 1, 8, rows), F32),
            pltpu.VMEM((Z, 8, rows), F32),
            pltpu.SemaphoreType.DMA,
            pltpu.SemaphoreType.DMA((160,)),
            pltpu.SemaphoreType.DMA((160,)),
        ]

    def peer(self, axis, d):
        z, x, y, c = self.z, self.x, self.y, self.c
        if axis == "z":
            z = lax.rem(z + d, self.Z)
        elif axis == "x":
            x = lax.rem(x + d, self.X)
        elif axis == "y":
            y = lax.rem(y + d, self.Y)
        else:
            c = 1 - c
        return (z, (x * self.Y + y) * self.C + c)

    def send(self, src, dst, axis, d):
        i = self.sems
        self.sems += 1
        copy = pltpu.make_async_remote_copy(
            src_ref=src,
            dst_ref=dst,
            send_sem=self.send_sem.at[i],
            recv_sem=self.recv_sem.at[i],
            device_id=self.peer(axis, d),
            device_id_type=MESH,
        )
        copy.start()
        self.sent.append(copy)
        return copy

    def row_part(self, x, c=None):
        c = self.c if c is None else c
        return pl.ds(pl.multiple_of(c * self.half + x * self.part, self.part), self.part)

    def x_part(self, x):
        return pl.ds(pl.multiple_of(x * self.part, self.part), self.part)

    def core_half(self, c):
        return pl.ds(pl.multiple_of(c * self.half, self.half), self.half)

    def y_cols(self, y):
        return pl.ds(pl.multiple_of(y * self.col, self.col), self.col)

    def z_cols(self, z):
        return pl.ds(pl.multiple_of(z * self.code_col, self.code_col), self.code_col)

    def reduce_scatter(self, bufs, hooks):
        part_sum, got_core, core_sum, got_x, x_sum, got_y = bufs
        X, Y = self.X, self.Y
        cp = self.send(part_sum.at[self.core_half(1 - self.c)], got_core, "c", 1)
        hooks[0]()
        cp.wait_recv()
        copies = []
        for d in far_first(X) + [0]:
            xx = lax.rem(self.x + d, X)
            core_sum[self.x_part(xx), :] = part_sum[self.row_part(xx), :] + got_core[self.x_part(xx), :]
            if d:
                copies.append(self.send(core_sum.at[self.x_part(xx)], got_x.at[d - 1], "x", d))
        hooks[1]()
        for cp in copies:
            cp.wait_recv()
        total = core_sum[self.x_part(self.x), :]
        for d in range(1, X):
            total += got_x[d - 1]
        x_sum[...] = total
        copies = [
            self.send(x_sum.at[:, self.y_cols(lax.rem(self.y + d, Y))], got_y.at[d - 1], "y", d)
            for d in far_first(Y)
        ]
        hooks[2]()
        for cp in copies:
            cp.wait_recv()
        total = x_sum[:, self.y_cols(self.y)]
        for d in range(1, Y):
            total += got_y[d - 1]
        return total

    def gather_y(self, dst):
        own = (self.row_part(self.x), self.y_cols(self.y))
        return [self.send(dst.at[own], dst.at[own], "y", d) for d in far_first(self.Y)]

    def gather_x(self, pieces):
        return [(d, [self.send(p, p, "x", d) for p in pieces]) for d in far_first(self.X)]

    def to_core(self, piece):
        return self.send(piece, piece, "c", 1)

    def forward_x(self, got, pieces_of):
        out = []
        for d, copies in got:
            for cp in copies:
                cp.wait_recv()
            xx = lax.rem(self.x + self.X - d, self.X)
            out += [self.to_core(p) for p in pieces_of(xx)]
        return out

    def __call__(
        self, u_hbm, hid_ref, down_ref, meta_ref, loss_ref, gh_ref, gd_ref, gu_ref,
        u, dn, hid, meta,
        p1, p1c, p1s, p1x, p1t, p1y,
        p2, p2c, p2s, p2x, p2t, p2y,
        codes, gcode, gcol, logit, gt, g, acc, st, st_c, st_x, st_y, fin,
        u_sem, send_sem, recv_sem,
    ):
        X, Y, C, Z = self.X, self.Y, self.C, self.Z
        rows, rank, vocab = self.rows, self.rank, self.vocab
        self.send_sem, self.recv_sem, self.sent, self.sems = send_sem, recv_sem, [], 0
        self.z = lax.axis_index("feat")
        v = lax.axis_index("vocab")
        self.x, self.y, self.c = v // (Y * C), lax.rem(v // C, Y), lax.rem(v, C)
        z, c = self.z, self.c
        tiles = vocab // TILE

        u_copy = pltpu.make_async_copy(u_hbm, u, u_sem)
        u_copy.start()
        barrier = pltpu.get_barrier_semaphore()
        partners = [(a, d) for a, n in zip("xyz", (X, Y, Z)) for d in range(1, n)] + [("c", 1)]
        for a, d in partners:
            pl.semaphore_signal(barrier, inc=1, device_id=self.peer(a, d), device_id_type=MESH)
        pl.semaphore_wait(barrier, len(partners))

        downs = [self.send(down_ref, dn.at[:, self.z_cols(z)], "z", d) for d in far_first(Z)]
        others = [self.send(hid_ref, hid.at[Z - d], "z", d) for d in far_first(Z)]
        metas = [self.send(meta_ref, meta.at[Z - d], "z", d) for d in far_first(Z)]
        dn[:, self.z_cols(z)] = down_ref[...]
        hid[0] = hid_ref[...]
        meta[0] = meta_ref[...]
        acc[...] = jnp.zeros_like(acc)
        for cp in downs:
            cp.wait_recv()
        p1[...] = jnp.dot(hid_ref[...], dn[...], preferred_element_type=F32)
        idle = lambda: None
        block = self.reduce_scatter((p1, p1c, p1s, p1x, p1t, p1y), (idle, idle, idle))

        own = codes.at[0]
        own[self.row_part(self.x), self.y_cols(self.y)] = block.astype(BF16)
        for cp in self.gather_y(own):
            cp.wait_recv()
        got = self.gather_x([own.at[self.row_part(self.x)]])
        cores = [self.to_core(own.at[self.row_part(self.x)])]
        cores += self.forward_x(got, lambda xx: [own.at[self.row_part(xx)]])

        ring = {}

        def quarter(right):
            n = self.half // 2
            return pl.ds(pl.multiple_of(c * self.half + (0 if right else n), n), n)

        def ring_send(s):
            last = s == Z // 2
            copies = []
            for right in (True, False):
                src = (Z - (s - 1)) % Z if right else s - 1
                dst = Z - s if right else s
                part = quarter(right) if last else self.core_half(c)
                copies.append(self.send(codes.at[src, part], codes.at[dst, part], "z", 1 if right else Z - 1))
            ring[s] = copies

        handed = {}

        def ring_step(s):
            for cp in ring[s]:
                cp.wait_recv()
            if s < Z // 2:
                ring_send(s + 1)
                for slot in (Z - s, s):
                    handed[slot] = self.to_core(codes.at[slot, self.core_half(c)])
            else:
                handed[s] = self.to_core(codes.at[s, self.core_half(c)])

        ring_send(1)
        for cp in cores:
            cp.wait_recv()

        u_copy.wait()

        def logit_tile(i, peak):
            at = pl.ds(pl.multiple_of(i * TILE, TILE), TILE)
            l = lax.dot_general(u[at, :], own[...], NT, preferred_element_type=F32)
            logit[at, :] = l
            return jnp.maximum(peak, jnp.max(l, axis=0, keepdims=True))

        low = jnp.full((1, rows), -jnp.inf, F32)
        peak = lax.fori_loop(0, tiles, logit_tile, low)
        first = v * vocab
        scale = meta_ref[1:2, :]

        def hits(i, slot):
            at = lax.broadcasted_iota(jnp.int32, (TILE, rows), 0) + (first + i * TILE)
            return at == meta[slot, 0:1, :].astype(jnp.int32)

        def exp_tile(i, carry):
            total, picked = carry
            at = pl.ds(pl.multiple_of(i * TILE, TILE), TILE)
            l = logit[at, :]
            picked += jnp.sum(jnp.where(hits(i, 0), l, 0.0), axis=0, keepdims=True)
            e = jnp.exp(l - peak)
            logit[at, :] = e
            return total + jnp.sum(e, axis=0, keepdims=True), picked

        none = jnp.zeros((1, rows), F32)
        total, picked = lax.fori_loop(0, tiles, exp_tile, (none, none))

        def put(ref, a, b, d):
            ref[0:1, :], ref[1:2, :], ref[2:3, :] = a, b, d

        def merge(stats):
            top = functools.reduce(jnp.maximum, [s[0] for s in stats])
            return (
                top,
                sum(s[1] * jnp.exp(s[0] - top) for s in stats),
                sum(s[2] for s in stats),
            )

        def take(ref):
            return ref[0:1, :], ref[1:2, :], ref[2:3, :]

        mine = (peak, total, picked)
        st[...] = jnp.zeros_like(st)
        for k, (axis, n, got) in enumerate((("c", C, [st_c]), ("x", X, None), ("y", Y, None))):
            if got is None:
                buf = st_x if axis == "x" else st_y
                got = [buf.at[d - 1] for d in range(1, n)]
            put(st.at[k], *mine)
            copies = [self.send(st.at[k], got[d - 1], axis, d) for d in far_first(n)]
            if k == 2:
                ring_step(1)
            for cp in copies:
                cp.wait_recv()
            mine = merge([mine] + [take(r) for r in got])
        top, total, picked = mine
        loss_ref[...] = jnp.broadcast_to(top + jnp.log(total) - picked, loss_ref.shape)
        weight = scale / total
        fin[0] = jnp.zeros((8, rows), F32)
        put(fin.at[0], top, weight, picked)
        finals = [self.send(fin.at[0], fin.at[Z - d], "z", d) for d in far_first(Z)]

        shrink = jnp.exp(peak - top) * weight

        def grad_tile(i, _):
            at = pl.ds(pl.multiple_of(i * TILE, TILE), TILE)
            grad = logit[at, :] * shrink - jnp.where(hits(i, 0), scale, 0.0)
            gt[at, :] = grad.astype(BF16)
            g[:, at] = grad.T.astype(BF16)
            return 0

        lax.fori_loop(0, tiles, grad_tile, 0)
        wide = min(256, rank)

        def code_tile(i, _):
            at = pl.ds(pl.multiple_of(i * wide, wide), wide)
            p2[:, at] = jnp.dot(g[...], u[:, at], preferred_element_type=F32)
            return 0

        lax.fori_loop(0, rank // wide, code_tile, 0)

        def own_plane():
            def tile(i, _):
                at = pl.ds(pl.multiple_of(i * TILE, TILE), TILE)
                acc[at, :] += jnp.dot(gt[at, :], codes[0, :, self.z_cols(z)], preferred_element_type=F32)
                return 0

            lax.fori_loop(0, tiles, tile, 0)

        def plane(slot):
            handed[slot].wait_recv()
            top, weight = fin[slot, 0:1, :], fin[slot, 1:2, :]

            def tile(i, _):
                at = pl.ds(pl.multiple_of(i * TILE, TILE), TILE)
                l = lax.dot_general(u[at, :], codes[slot], NT, preferred_element_type=F32)
                grad = jnp.exp(l - top) * weight - jnp.where(hits(i, slot), scale, 0.0)
                acc[at, :] += jnp.dot(
                    grad.astype(BF16), codes[slot, :, self.z_cols(z)], preferred_element_type=F32
                )
                return 0

            lax.fori_loop(0, tiles, tile, 0)

        def ready():
            for cp in finals + metas + others:
                cp.wait_recv()

        steps = [lambda s=s: ring_step(s) for s in range(2, Z // 2 + 1)]
        planes = [s for d in range(1, Z // 2) for s in (Z - d, d)] + [Z // 2]
        todo = {k: [] for k in range(8)}
        todo[0] = [own_plane]
        todo[1] = steps[0:1] + [ready] + [lambda s=s: plane(s) for s in planes[0:2]]
        todo[2] = steps[1:2] + [lambda s=s: plane(s) for s in planes[2:3]]
        todo[3] = steps[2:3] + [lambda s=s: plane(s) for s in planes[3:4]]
        todo[4] = [lambda s=s: plane(s) for s in planes[4:5]]
        todo[5] = [lambda s=s: plane(s) for s in planes[5:6]]
        todo[6] = [lambda s=s: plane(s) for s in planes[6:7]]

        def work(k):
            for item in todo[k]:
                item()

        hooks = tuple(lambda k=k: work(k) for k in range(3))
        block = self.reduce_scatter((p2, p2c, p2s, p2x, p2t, p2y), hooks)
        here = self.row_part(self.x)
        gcode[here, self.y_cols(self.y)] = block.astype(BF16)
        got = self.gather_y(gcode)
        work(3)
        for cp in got:
            cp.wait_recv()
        got = self.gather_x([gcode.at[here]])
        cols = [
            self.send(
                gcode.at[here, self.z_cols(lax.rem(z + d, Z))], gcol.at[Z - d, here], "z", d
            )
            for d in far_first(Z)
        ]
        cores = [self.to_core(gcode.at[here])]
        work(4)
        for cp in cols:
            cp.wait_recv()
        got_cols = self.gather_x([gcol.at[pl.ds(1, Z - 1), here]])
        cores += [self.to_core(gcol.at[pl.ds(1, Z - 1), here])]
        cores += self.forward_x(got, lambda xx: [gcode.at[self.row_part(xx)]])
        work(5)
        cores += self.forward_x(got_cols, lambda xx: [gcol.at[pl.ds(1, Z - 1), self.row_part(xx)]])
        work(6)
        gu_ref[...] = acc[...].astype(BF16)
        for cp in cores:
            cp.wait_recv()
        gh_ref[...] = lax.dot_general(gcode[...], dn[...], NT, preferred_element_type=F32)
        down = lax.dot_general(hid[0], gcode[:, self.z_cols(z)], TN, preferred_element_type=F32)
        for s in range(1, Z):
            down += lax.dot_general(hid[s], gcol[s], TN, preferred_element_type=F32)
        gd_ref[...] = down
        for cp in self.sent:
            cp.wait_send()


def build(mesh, dims):
    def shards(hidden, down_factor, unembed, targets, depth_scale):
        depth, some, width = hidden.shape
        rows, (vocab, rank) = depth * some, unembed.shape
        meta = jnp.stack(
            [
                targets.astype(F32).reshape(rows),
                jnp.repeat(depth_scale, some),
                *[jnp.zeros((rows,), F32)] * 6,
            ]
        )
        kernel = Kernel(dims, rows, rank, width, vocab)
        vmem = pl.BlockSpec(memory_space=pltpu.VMEM)
        code_col = rank // dims[3]
        loss, gh, gd, gu = pl.pallas_call(
            kernel.__call__,
            out_shape=(
                jax.ShapeDtypeStruct((8, rows), F32),
                jax.ShapeDtypeStruct((rows, width), F32),
                jax.ShapeDtypeStruct((width, code_col), F32),
                jax.ShapeDtypeStruct((vocab, code_col), BF16),
            ),
            in_specs=[pl.BlockSpec(memory_space=pl.ANY), vmem, vmem, vmem],
            out_specs=(vmem,) * 4,
            scratch_shapes=kernel.scratch(),
            compiler_params=pltpu.CompilerParams(
                collective_id=0, has_side_effects=True, vmem_limit_bytes=56 << 20
            ),
            name="fused",
        )(unembed, hidden.reshape(rows, width), down_factor, meta)
        return loss[0].reshape(depth, some), gh.reshape(depth, some, width), gd, gu

    placed = (P(None, "feat", "vocab"), P("vocab", "feat"), P("vocab", None), P(None, "feat"), P())
    return jax.shard_map(
        shards,
        mesh=mesh,
        in_specs=placed,
        out_specs=(
            P(None, "feat"),
            P(None, "feat", "vocab"),
            P("vocab", "feat"),
            P("vocab", "feat"),
        ),
        check_vma=False,
    )


def solution(mesh):
    return build(mesh, (4, 8, 2, 8))
```

time: 885 us -> 109 us (0.12); the launches traced: 871 us -> 109 us
  blocking collectives: 812 us -> 0 us
  Pallas kernels: 0 us -> 99.3 us
  matrix products: 16.9 us -> 0 us
  between operations: 14.2 us -> 0.65 us
  waiting for transfers between devices: 10.1 us -> 0 us
    psum x3 -> x0, blocking collectives: 632 us -> none  [the longest x2 377 us: shards(): total, picked = lax.psum((local_total, target_part), 'vocab')]
    pmax x1 -> x0, blocking collectives: 129 us -> none  [shards(): peak = lax.pmax(local_peak, 'vocab')]
    pallas_call x0 -> x1, Pallas kernels: none -> 99.3 us  [shards(): pl.pallas_call(kernel.__call__, out_shape=(jax.ShapeDtypeStruct((8, rows)...]
    all_gather x2 -> x0, blocking collectives: 50.7 us -> none  [the longest x1 26.1 us: shards(): lax.all_gather(hidden, 'feat', axis=1, tiled=True)]
    dot_general x6 -> x0, matrix products: 16.9 us -> none  [the longest x1 6.58 us: shards(): jnp.einsum('krv,krc->vc', lax.all_gather(grad_logits, 'feat', axis=1, til...]
    all_to_all x2 -> x0, waiting for transfers between devices: 10.1 us -> none  [the longest x1 10.1 us: shards(): lax.all_to_all(grad_codes, 'feat', split_axis=2, concat_axis=1, tiled=True)]
  transfers between devices with their start and end apart: 3 -> 0, of which waited for: 1 -> 0; matrix products, arithmetic and copies ran while one was open for 2% -> 0% of each run, Pallas kernels for 0% -> 0%
where the time goes in v1:
time: 109 us
  Pallas kernels  99.3 us (91%)
  local copies, waits for them, and re-layouts  7.3 us (7%)
  other arithmetic  1.36 us (1%)
    pallas_call x1, Pallas kernels, shards(): pl.pallas_call(kernel.__call__, out_shape=(jax.ShapeDtypeStruct((8, rows)...  99.3 us
    unnamed x3, local copies, waits for them, and re-layouts  4.88 us

profile of v1, /device:TPU:1, one launch (start us, length us, event | category | flops | bytes accessed | tf_op | source)
XLA Modules:
  0.0 108.6 jit_solution(95312891532288626)
XLA Ops:
  0.6 0.1 pad.3.clone
  0.7 0.1 pad.2.clone
  0.8 0.7 convert_element_type.3
  1.5 0.1 stack_reshape.6
  1.6 0.7 broadcast_in_dim.3
  2.3 0.1 stack_reshape.7
  2.4 0.7 maximum_maximum_fusion.meta_ref
  3.0 99.3 %fused.1 = (f32[8,256]{1,0:T(8,128)}, f32[256,112]{1,0:T(8,128)}, f32[112,128]{1,0:T(8,128)}, bf16[2048,128]{1,0:T(8,128)(2,1)}) custom-call(bf16[2048,1024]{1,0:T(8,128)(2,1)} %u_hbm.1, bf16[256,112]{1,0:T(8,128)(2,1)} %bitcast.3, bf16[112,128]{1,0:T(8,128)(2,1)} %down_ref.1, f32[8,256]{1,0:T(8,128)} %maximum_maximum_fusion.meta_ref), custom_call_target="tpu_custom_call" | custom-call | tf_op jit(solution)/shard_map/fused/pallas_call | solution.py:415
  102.4 0.7 slice_reduce_fusion
  103.1 0.7 reshape_squeeze.3
  103.8 1.6 %copy.12 = f32[4,64,112]{2,1,0:T(8,128)} copy(f32[4,64,112]{2,1,0:T(8,128)} %bitcast.2) | data formatting | bytes 229376
  105.3 1.4 %copy.13 = f32[112,128]{1,0:T(8,128)} copy(f32[112,128]{1,0:T(8,128)} %get-tuple-element.18) | data formatting | bytes 114688
  106.8 1.9 %copy.14 = bf16[2048,128]{1,0:T(8,128)(2,1)} copy(bf16[2048,128]{1,0:T(8,128)(2,1)} %get-tuple-element.19) | data formatting | bytes 1048576
  (2 shorter events, 0.0 us)

commit v2 on v1

v2 whole, which is shorter than its diff:
```python
import functools

import jax
import jax.numpy as jnp
from jax import lax
from jax.experimental import pallas as pl
from jax.experimental.pallas import tpu as pltpu
from jax.sharding import PartitionSpec as P

MESH = pl.DeviceIdType.MESH
F32, BF16 = jnp.float32, jnp.bfloat16
TILE = 1024
WIDE = 512
NT = (((1,), (1,)), ((), ()))
TN = (((0,), (0,)), ((), ()))


def far_first(n):
    return sorted(range(1, n), key=lambda d: -min(d, n - d))


class Kernel:
    def __init__(self, dims, rows, rank, width, vocab):
        self.X, self.Y, self.C, self.Z = dims
        self.rows, self.rank, self.width, self.vocab = rows, rank, width, vocab
        self.half = rows // self.C
        self.part = self.half // self.X
        self.col = rank // self.Y
        self.code_col = rank // self.Z
        self.sems = 0

    def scratch(self):
        X, Y, Z = self.X, self.Y, self.Z
        rows, rank, half, part, col = self.rows, self.rank, self.half, self.part, self.col

        def reduce_set(kind):
            return [
                pltpu.VMEM((rows, rank), kind),
                pltpu.VMEM((half, rank), kind),
                pltpu.VMEM((half, rank), kind),
                pltpu.VMEM((X - 1 or 1, part, rank), kind),
                pltpu.VMEM((part, rank), kind),
                pltpu.VMEM((Y - 1 or 1, part, col), kind),
            ]

        return [
            pltpu.VMEM((self.vocab, rank), BF16),
            pltpu.VMEM((self.width, rank), BF16),
            pltpu.VMEM((Z, rows, self.width), BF16),
            pltpu.VMEM((Z, 8, rows), F32),
            *reduce_set(F32),
            *reduce_set(F32),
            *reduce_set(BF16),
            pltpu.VMEM((Z, rows, rank), BF16),
            pltpu.VMEM((rows, rank), BF16),
            pltpu.VMEM((Z, rows, self.code_col), BF16),
            pltpu.VMEM((Z, self.vocab, rows), F32),
            pltpu.VMEM((rows, self.vocab), BF16),
            pltpu.VMEM((self.vocab, self.code_col), F32),
            pltpu.VMEM((3, 8, rows), F32),
            pltpu.VMEM((8, rows), F32),
            pltpu.VMEM((X - 1 or 1, 8, rows), F32),
            pltpu.VMEM((Y - 1 or 1, 8, rows), F32),
            pltpu.VMEM((Z, 8, rows), F32),
            pltpu.VMEM((4, rows, 8), F32),
            pltpu.VMEM((4, rows // 4), jnp.int32),
            pltpu.SemaphoreType.DMA((4,)),
            pltpu.SemaphoreType.DMA((160,)),
            pltpu.SemaphoreType.DMA((160,)),
        ]

    def peer(self, axis, d):
        z, x, y, c = self.z, self.x, self.y, self.c
        if axis == "z":
            z = lax.rem(z + d, self.Z)
        elif axis == "x":
            x = lax.rem(x + d, self.X)
        elif axis == "y":
            y = lax.rem(y + d, self.Y)
        else:
            c = 1 - c
        return (z, (x * self.Y + y) * self.C + c)

    def send(self, src, dst, axis, d):
        i = self.sems
        self.sems += 1
        copy = pltpu.make_async_remote_copy(
            src_ref=src,
            dst_ref=dst,
            send_sem=self.send_sem.at[i],
            recv_sem=self.recv_sem.at[i],
            device_id=self.peer(axis, d),
            device_id_type=MESH,
        )
        copy.start()
        self.sent.append(copy)
        return copy

    def row_part(self, x, c=None):
        c = self.c if c is None else c
        return pl.ds(pl.multiple_of(c * self.half + x * self.part, self.part), self.part)

    def x_part(self, x):
        return pl.ds(pl.multiple_of(x * self.part, self.part), self.part)

    def core_half(self, c):
        return pl.ds(pl.multiple_of(c * self.half, self.half), self.half)

    def y_cols(self, y):
        return pl.ds(pl.multiple_of(y * self.col, self.col), self.col)

    def z_cols(self, z):
        return pl.ds(pl.multiple_of(z * self.code_col, self.code_col), self.code_col)

    def sum_core(self, bufs, a=None, b=None):
        part_sum, got_core, core_sum = bufs[:3]
        copies = []
        for d in far_first(self.X) + [0]:
            xx = lax.rem(self.x + d, self.X)
            at, wide = self.x_part(xx), self.row_part(xx)
            if a is None:
                core_sum[at, :] = part_sum[wide, :] + got_core[at, :]
            else:
                core_sum[at, :] = part_sum[wide, :] * a[wide, 0:1] + got_core[at, :] * b[wide, 1:2]
            if d:
                copies.append(self.send(core_sum.at[at], bufs[3].at[d - 1], "x", d))
        return copies

    def sum_x(self, bufs, w=None):
        core_sum, got_x, x_sum, got_y = bufs[2:]
        total = core_sum[self.x_part(self.x), :]
        here = self.row_part(self.x)
        if w is not None:
            total *= w[here, 0:1]
        for d in range(1, self.X):
            total += got_x[d - 1] if w is None else got_x[d - 1] * w[here, d : d + 1]
        x_sum[...] = total
        return [
            self.send(x_sum.at[:, self.y_cols(lax.rem(self.y + d, self.Y))], got_y.at[d - 1], "y", d)
            for d in far_first(self.Y)
        ]

    def sum_y(self, bufs, w=None):
        x_sum, got_y = bufs[4:]
        total = x_sum[:, self.y_cols(self.y)]
        here = self.row_part(self.x)
        if w is not None:
            total *= w[here, 0:1]
        for d in range(1, self.Y):
            total += got_y[d - 1] if w is None else got_y[d - 1] * w[here, d : d + 1]
        return total

    def gather_y(self, dst):
        own = (self.row_part(self.x), self.y_cols(self.y))
        return [self.send(dst.at[own], dst.at[own], "y", d) for d in far_first(self.Y)]

    def gather_x(self, pieces):
        return [(d, [self.send(p, p, "x", d) for p in pieces]) for d in far_first(self.X)]

    def to_core(self, piece):
        return self.send(piece, piece, "c", 1)

    def forward_x(self, got, pieces_of):
        out = []
        for d, copies in got:
            for cp in copies:
                cp.wait_recv()
            xx = lax.rem(self.x + self.X - d, self.X)
            out += [self.to_core(p) for p in pieces_of(xx)]
        return out

    def __call__(
        self, u_hbm, hid_hbm, down_hbm, target_hbm, scale_ref, loss_out, gh_out, gd_out, gu_out,
        u, dn, hid, meta,
        p1, p1c, p1s, p1x, p1t, p1y,
        p2, p2c, p2s, p2x, p2t, p2y,
        p3, p3c, p3s, p3x, p3t, p3y,
        codes, gcode, gcol, logit, g, acc, st, st_c, st_x, st_y, fin, weights,
        target,
        local_sem, send_sem, recv_sem,
    ):
        X, Y, C, Z = self.X, self.Y, self.C, self.Z
        rows, rank, vocab = self.rows, self.rank, self.vocab
        self.send_sem, self.recv_sem, self.sent, self.sems = send_sem, recv_sem, [], 0
        self.z = lax.axis_index("feat")
        v = lax.axis_index("vocab")
        self.x, self.y, self.c = v // (Y * C), lax.rem(v // C, Y), lax.rem(v, C)
        z, c = self.z, self.c
        tiles = vocab // TILE

        def local(src, dst, i):
            copy = pltpu.make_async_copy(src, dst, local_sem.at[i])
            copy.start()
            return copy

        down_slot = dn.at[:, self.z_cols(z)]
        loads = [
            local(down_hbm, down_slot, 0),
            local(hid_hbm, hid.at[0], 1),
            local(target_hbm, target, 2),
        ]
        u_copy = local(u_hbm, u, 3)
        self.u_copy, self.loads = u_copy, loads
        barrier = pltpu.get_barrier_semaphore()
        partners = [(a, d) for a, n in zip("xyz", (X, Y, Z)) for d in range(1, n)] + [("c", 1)]
        for a, d in partners:
            pl.semaphore_signal(barrier, inc=1, device_id=self.peer(a, d), device_id_type=MESH)
        pl.semaphore_wait(barrier, len(partners))

        for cp in loads:
            cp.wait()
        downs = [self.send(down_slot, down_slot, "z", d) for d in far_first(Z)]
        acc[...] = jnp.zeros_like(acc)
        meta[0] = jnp.zeros((8, rows), F32)
        some, lanes = rows // 4, rows // 2
        flat = jnp.concatenate([target[...].astype(F32), jnp.zeros((4, some), F32)], axis=1)
        turned = pltpu.roll(flat, some, axis=1)
        left = lax.broadcasted_iota(jnp.int32, (1, lanes), 1) < some
        for i in range(2):
            at = slice(i * lanes, (i + 1) * lanes)
            meta[0, 0:1, at] = jnp.where(left, flat[2 * i : 2 * i + 1], turned[2 * i + 1 : 2 * i + 2])
            meta[0, 1:2, at] = jnp.where(left, scale_ref[2 * i], scale_ref[2 * i + 1])
        first = v * vocab
        u_copy.wait()
        column = jnp.transpose(meta[0])[:, 0:1].astype(jnp.int32) - first

        def target_tile(i, _):
            at = pl.ds(pl.multiple_of(i * WIDE, WIDE), WIDE)
            place = lax.broadcasted_iota(jnp.int32, (rows, vocab), 1)
            one = jnp.where(place == column, 1.0, 0.0).astype(BF16)
            p3[:, at] = jnp.dot(one, u[:, at], preferred_element_type=F32).astype(BF16)
            return 0

        lax.fori_loop(0, rank // WIDE, target_tile, 0)
        mine3, theirs3 = self.core_half(c), self.core_half(1 - c)
        b1 = (p1, p1c, p1s, p1x, p1t, p1y)
        b2 = (p2, p2c, p2s, p2x, p2t, p2y)
        b3 = (p3, p3c, p3s, p3x, p3t, p3y)
        core3 = self.send(p3.at[theirs3], p3c, "c", 1)
        for cp in downs:
            cp.wait_recv()
        p1[theirs3, :] = jnp.dot(hid[0, theirs3], dn[...], preferred_element_type=F32)
        core1 = self.send(p1.at[theirs3], p1c, "c", 1)
        p1[mine3, :] = jnp.dot(hid[0, mine3], dn[...], preferred_element_type=F32)
        others = [self.send(hid.at[0], hid.at[Z - d], "z", d) for d in far_first(Z)]
        metas = [self.send(meta.at[0], meta.at[Z - d], "z", d) for d in far_first(Z)]
        core1.wait_recv()
        got1 = self.sum_core(b1)
        core3.wait_recv()
        for cp in got1:
            cp.wait_recv()
        got1 = self.sum_x(b1)
        got3 = self.sum_core(b3)
        for cp in got1:
            cp.wait_recv()
        block = self.sum_y(b1)
        own = codes.at[0]
        own[self.row_part(self.x), self.y_cols(self.y)] = block.astype(BF16)
        for cp in self.gather_y(own):
            cp.wait_recv()
        got = self.gather_x([own.at[self.row_part(self.x)]])
        cores = [self.to_core(own.at[self.row_part(self.x)])]
        cores += self.forward_x(got, lambda xx: [own.at[self.row_part(xx)]])

        ring = {}

        def quarter(right):
            n = self.half // 2
            return pl.ds(pl.multiple_of(c * self.half + (0 if right else n), n), n)

        def ring_send(s):
            last = s == Z // 2
            copies = []
            for right in (True, False):
                src = (Z - (s - 1)) % Z if right else s - 1
                dst = Z - s if right else s
                part = quarter(right) if last else self.core_half(c)
                copies.append(self.send(codes.at[src, part], codes.at[dst, part], "z", 1 if right else Z - 1))
            ring[s] = copies

        handed = {}

        def ring_step(s):
            for cp in ring[s]:
                cp.wait_recv()
            if s < Z // 2:
                ring_send(s + 1)
                for slot in (Z - s, s):
                    handed[slot] = self.to_core(codes.at[slot, self.core_half(c)])
            else:
                handed[s] = self.to_core(codes.at[s, self.core_half(c)])

        ring_send(1)
        for cp in cores:
            cp.wait_recv()

        def logit_tile(slot, i):
            at = pl.ds(pl.multiple_of(i * TILE, TILE), TILE)
            l = lax.dot_general(u[at, :], codes[slot], NT, preferred_element_type=F32)
            logit[slot, at, :] = l
            return l

        low = jnp.full((1, rows), -jnp.inf, F32)
        peak = lax.fori_loop(
            0,
            tiles,
            lambda i, m: jnp.maximum(m, jnp.max(logit_tile(0, i), axis=0, keepdims=True)),
            low,
        )
        scale = meta[0, 1:2, :]

        def hits(i, slot):
            at = lax.broadcasted_iota(jnp.int32, (TILE, rows), 0) + (first + i * TILE)
            return at == meta[slot, 0:1, :].astype(jnp.int32)

        def exp_tile(i, carry):
            total, picked = carry
            at = pl.ds(pl.multiple_of(i * TILE, TILE), TILE)
            l, hit = logit[0, at, :], hits(i, 0)
            picked += jnp.sum(jnp.where(hit, l, 0.0), axis=0, keepdims=True)
            e = jnp.exp(l - peak)
            g[:, at] = jnp.where(hit, 0.0, e).T.astype(BF16)
            return total + jnp.sum(e, axis=0, keepdims=True), picked

        none = jnp.zeros((1, rows), F32)
        total, picked = lax.fori_loop(0, tiles, exp_tile, (none, none))

        def put(ref, a, b, d):
            ref[0:1, :], ref[1:2, :], ref[2:3, :] = a, b, d

        def take(ref):
            return ref[0:1, :], ref[1:2, :], ref[2:3, :]

        def columns(k, values):
            values = list(values) + [none] * (8 - len(values))
            weights[k] = jnp.transpose(jnp.concatenate(values, axis=0))

        def merge(k, stats):
            top = functools.reduce(jnp.maximum, [s[0] for s in stats])
            w = [jnp.exp(s[0] - top) for s in stats]
            columns(k, w)
            return top, sum(s[1] * f for s, f in zip(stats, w)), sum(s[2] for s in stats)

        def swap(k, axis, n, got):
            put(st.at[k], *mine)
            return [self.send(st.at[k], got(d), axis, d) for d in far_first(n)]

        def got_all(copies):
            for cp in copies:
                cp.wait_recv()

        st[...] = jnp.zeros_like(st)
        fin[0] = jnp.zeros((8, rows), F32)
        mine = (peak, total, picked)
        stats = swap(0, "c", C, lambda d: st_c)
        core2 = []
        for i in range(rank // WIDE):
            at = pl.ds(i * WIDE, WIDE)
            p2[:, at] = jnp.dot(g[...], u[:, at], preferred_element_type=F32)
            core2.append(self.send(p2.at[theirs3, at], p2c.at[:, at], "c", 1))
        got_all(stats)
        mine = merge(0, [mine, take(st_c)])
        stats = swap(1, "x", X, lambda d: st_x.at[d - 1])

        def logits_of(slot):
            handed[slot].wait_recv()
            lax.fori_loop(0, tiles, lambda i, _: (logit_tile(slot, i), 0)[1], 0)

        def gradient_of(slot):
            top, weight = fin[slot, 0:1, :], fin[slot, 1:2, :]

            def tile(i, _):
                at = pl.ds(pl.multiple_of(i * TILE, TILE), TILE)
                e = jnp.exp(logit[slot, at, :] - top) * weight
                grad = e - jnp.where(hits(i, slot), scale, 0.0)
                acc[at, :] += jnp.dot(
                    grad.astype(BF16), codes[slot, :, self.z_cols(z)], preferred_element_type=F32
                )
                return 0

            lax.fori_loop(0, tiles, tile, 0)

        got_all(core2)
        got2 = self.sum_core(b2, weights.at[0], weights.at[0])
        got_all(got3)
        got3 = self.sum_x(b3)
        ring_step(1)
        got_all(stats)
        mine = merge(1, [mine] + [take(st_x.at[d - 1]) for d in range(1, X)])
        stats = swap(2, "y", Y, lambda d: st_y.at[d - 1])
        planes = [s for d in range(1, Z // 2) for s in (Z - d, d)] + [Z // 2]
        early = planes[:4] if Z > 4 else planes[:1]
        late = [s for s in planes if s not in early]
        for s in early[:2]:
            logits_of(s)
        got_all(got2)
        got2 = self.sum_x(b2, weights.at[1])
        got_all(stats)
        top, total, picked = merge(2, [mine] + [take(st_y.at[d - 1]) for d in range(1, Y)])
        weight = scale / total
        put(fin.at[0], top, weight, picked)
        finals = [self.send(fin.at[0], fin.at[Z - d], "z", d) for d in far_first(Z)]
        hit_grad = (scale * (jnp.exp(picked - top) / total - 1.0)).astype(BF16).astype(F32)
        columns(3, [weight, hit_grad])
        loss = top + jnp.log(total) - picked
        for i in range(2):
            pair = jnp.broadcast_to(loss[:, i * lanes : (i + 1) * lanes], (8, lanes))
            loss_out[2 * i : 2 * i + 1, :] = pair[0:1, :some]
            loss_out[2 * i + 1 : 2 * i + 2, :] = pltpu.roll(pair, some, axis=1)[0:1, :some]
        if Z > 2:
            ring_step(2)
        for s in early[2:]:
            logits_of(s)
        got_all(got3)
        target_row = self.sum_y(b3)
        got_all(got2)
        here = self.row_part(self.x)
        block = self.sum_y(b2, weights.at[2]) * weights[3, here, 0:1]
        block += weights[3, here, 1:2] * target_row.astype(F32)
        gcode[here, self.y_cols(self.y)] = block.astype(BF16)
        got = self.gather_y(gcode)
        gradient_of(0)
        if Z > 4:
            ring_step(3)
        got_all(finals + metas + others)
        gradient_of(early[0])
        got_all(got)
        got = self.gather_x([gcode.at[here]])
        cols = [
            self.send(
                gcode.at[here, self.z_cols(lax.rem(z + d, Z))], gcol.at[Z - d, here], "z", d
            )
            for d in far_first(Z)
        ]
        cores = [self.to_core(gcode.at[here])]
        for s in early[1:3]:
            gradient_of(s)
        got_all(cols)
        got_cols = self.gather_x([gcol.at[pl.ds(1, Z - 1), here]])
        col_cores = [self.to_core(gcol.at[pl.ds(1, Z - 1), here])]
        cores += self.forward_x(got, lambda xx: [gcode.at[self.row_part(xx)]])
        if Z > 6:
            ring_step(4)
        for s in early[3:]:
            gradient_of(s)
        for s in late[:1]:
            logits_of(s)
            gradient_of(s)
        col_cores += self.forward_x(got_cols, lambda xx: [gcol.at[pl.ds(1, Z - 1), self.row_part(xx)]])
        got_all(cores)
        gh_out[...] = lax.dot_general(gcode[...], dn[...], NT, preferred_element_type=F32)
        gcol[0] = gcode[:, self.z_cols(z)]
        for s in late[1:]:
            logits_of(s)
            gradient_of(s)
        gu_out[...] = acc[...].astype(BF16)
        got_all(col_cores)
        gd_out[...] = lax.dot_general(
            hid[...].reshape(Z * rows, self.width),
            gcol[...].reshape(Z * rows, self.code_col),
            TN,
            preferred_element_type=F32,
        )
        for cp in self.sent:
            cp.wait_send()


def hand_over(*refs):
    srcs, dsts, sem = refs[:4], refs[4:8], refs[8]
    copies = [pltpu.make_async_copy(a, b, sem.at[i]) for i, (a, b) in enumerate(zip(srcs, dsts))]
    for cp in copies:
        cp.start()
    for cp in copies:
        cp.wait()


def build(mesh, dims):
    def shards(hidden, down_factor, unembed, targets, depth_scale):
        depth, some, width = hidden.shape
        rows, (vocab, rank) = depth * some, unembed.shape
        kernel = Kernel(dims, rows, rank, width, vocab)
        far = pl.BlockSpec(memory_space=pl.ANY)
        near = pl.BlockSpec(memory_space=pltpu.VMEM)
        code_col = rank // dims[3]
        shapes = (
            jax.ShapeDtypeStruct((depth, some), F32),
            jax.ShapeDtypeStruct((rows, width), F32),
            jax.ShapeDtypeStruct((width, code_col), F32),
            jax.ShapeDtypeStruct((vocab, code_col), BF16),
        )
        made = pl.pallas_call(
            kernel.__call__,
            out_shape=tuple(pltpu.VMEM(s.shape, s.dtype) for s in shapes),
            in_specs=[far] * 4 + [pl.BlockSpec(memory_space=pltpu.SMEM)],
            out_specs=(near,) * 4,
            scratch_shapes=kernel.scratch(),
            compiler_params=pltpu.CompilerParams(
                collective_id=0, has_side_effects=True, vmem_limit_bytes=58 << 20
            ),
            name="fused",
        )(unembed, hidden.reshape(rows, width), down_factor, targets, depth_scale)
        loss, gh, gd, gu = pl.pallas_call(
            hand_over,
            out_shape=shapes,
            in_specs=[near] * 4,
            out_specs=(far,) * 4,
            scratch_shapes=[pltpu.SemaphoreType.DMA((4,))],
            compiler_params=pltpu.CompilerParams(vmem_limit_bytes=4 << 20),
            name="results",
        )(*made)
        return loss, gh.reshape(depth, some, width), gd, gu

    placed = (P(None, "feat", "vocab"), P("vocab", "feat"), P("vocab", None), P(None, "feat"), P())
    return jax.shard_map(
        shards,
        mesh=mesh,
        in_specs=placed,
        out_specs=(
            P(None, "feat"),
            P(None, "feat", "vocab"),
            P("vocab", "feat"),
            P("vocab", "feat"),
        ),
        check_vma=False,
    )


def solution(mesh):
    return build(mesh, (4, 8, 2, 8))
```

time: 109 us -> 90.1 us (0.83)
  Pallas kernels: 99.3 us -> 89.3 us
  local copies, waits for them, and re-layouts: 7.3 us -> 0 us
  other arithmetic: 1.36 us -> 0 us
    pallas_call x1 -> x2, Pallas kernels: 99.3 us -> 89.3 us  [the longest x1 88.4 us: shards(): pl.pallas_call(kernel.__call__, out_shape=tuple((pltpu.VMEM(s.shape, s.dt...]
    unnamed x3 -> x0, local copies, waits for them, and re-layouts: 4.88 us -> none
where the time goes in v2:
time: 90.1 us; the launch traced here: 90 us
  Pallas kernels  89.3 us (99%)
    pallas_call x1, Pallas kernels, shards(): pl.pallas_call(kernel.__call__, out_shape=tuple((pltpu.VMEM(s.shape, s.dt...  88.4 us

profile of v2, /device:TPU:1, one launch (start us, length us, event | category | flops | bytes accessed | tf_op | source)
XLA Modules:
  0.0 90.0 jit_solution(12042917918846951817)
XLA Ops:
  0.6 88.4 %fused.1 = (f32[4,64]{1,0:T(4,128)S(1)}, f32[256,112]{1,0:T(8,128)S(1)}, f32[112,128]{1,0:T(8,128)S(1)}, bf16[2048,128]{1,0:T(8,128)(2,1)S(1)}) custom-call(bf16[2048,1024]{1,0:T(8,128)(2,1)} %u_hbm.1, bf16[256,112]{1,0:T(8,128)(2,1)} %bitcast.2, bf16[112,128]{1,0:T(8,128)(2,1)} %down_hbm.1, s32[4,64]{1,0:T(4,128)} %target_hbm.1, f32[4]{0:T(128)} %scale_ref.1), custom_call_target="tpu_custom_call" | custom-call | tf_op jit(solution)/shard_map/fused/pallas_call | solution.py:491
  89.1 0.9 results.1

commit v3 on v2

--- a/solution.py
+++ b/solution.py
@@ -11,12 +11,48 @@
 F32, BF16 = jnp.float32, jnp.bfloat16
 TILE = 1024
 WIDE = 512
+SEMS = 94
 NT = (((1,), (1,)), ((), ()))
 TN = (((0,), (0,)), ((), ()))
 
 
 def far_first(n):
     return sorted(range(1, n), key=lambda d: -min(d, n - d))
+
+
+class Group:
+    def __init__(self, kernel, sem, total):
+        self.kernel, self.sem, self.total, self.copies = kernel, sem, total, []
+
+    def copy(self, src, dst, peer):
+        return pltpu.make_async_remote_copy(
+            src_ref=src,
+            dst_ref=dst,
+            send_sem=self.kernel.send_sem.at[self.sem],
+            recv_sem=self.kernel.recv_sem.at[self.sem],
+            device_id=peer,
+            device_id_type=MESH,
+        )
+
+    def add(self, src, dst, axis, d):
+        self.peer = self.kernel.peer(axis, d)
+        self.copies.append(self.copy(src, dst, self.peer))
+        return self
+
+    def send(self, src, dst, axis, d):
+        self.add(src, dst, axis, d)
+        self.copies[-1].start()
+
+    def start(self):
+        for copy in self.copies:
+            copy.start()
+        return self
+
+    def wait_recv(self):
+        self.copy(self.total, self.total, self.peer).wait_recv()
+
+    def wait_send(self):
+        self.copy(self.total, self.total, self.peer).wait_send()
 
 
 class Kernel:
@@ -65,8 +101,9 @@
             pltpu.VMEM((4, rows, 8), F32),
             pltpu.VMEM((4, rows // 4), jnp.int32),
             pltpu.SemaphoreType.DMA((4,)),
-            pltpu.SemaphoreType.DMA((160,)),
-            pltpu.SemaphoreType.DMA((160,)),
+            pltpu.SemaphoreType.DMA((SEMS,)),
+            pltpu.SemaphoreType.DMA((SEMS,)),
+            pltpu.SemaphoreType.DMA((2,)),
         ]
 
     def peer(self, axis, d):
@@ -81,20 +118,17 @@
             c = 1 - c
         return (z, (x * self.Y + y) * self.C + c)
 
+    def group(self, total):
+        found = Group(self, self.sems, total)
+        self.sems += 1
+        self.sent.append(found)
+        return found
+
     def send(self, src, dst, axis, d):
-        i = self.sems
-        self.sems += 1
-        copy = pltpu.make_async_remote_copy(
-            src_ref=src,
-            dst_ref=dst,
-            send_sem=self.send_sem.at[i],
-            recv_sem=self.recv_sem.at[i],
-            device_id=self.peer(axis, d),
-            device_id_type=MESH,
-        )
-        copy.start()
-        self.sent.append(copy)
-        return copy
+        return self.group(dst).add(src, dst, axis, d).start()
+
+    def make(self, src, dst, axis, d):
+        return self.group(dst).add(src, dst, axis, d)
 
     def row_part(self, x, c=None):
         c = self.c if c is None else c
@@ -112,61 +146,79 @@
     def z_cols(self, z):
         return pl.ds(pl.multiple_of(z * self.code_col, self.code_col), self.code_col)
 
-    def sum_core(self, bufs, a=None, b=None):
-        part_sum, got_core, core_sum = bufs[:3]
-        copies = []
-        for d in far_first(self.X) + [0]:
-            xx = lax.rem(self.x + d, self.X)
-            at, wide = self.x_part(xx), self.row_part(xx)
-            if a is None:
-                core_sum[at, :] = part_sum[wide, :] + got_core[at, :]
-            else:
-                core_sum[at, :] = part_sum[wide, :] * a[wide, 0:1] + got_core[at, :] * b[wide, 1:2]
-            if d:
-                copies.append(self.send(core_sum.at[at], bufs[3].at[d - 1], "x", d))
-        return copies
-
-    def sum_x(self, bufs, w=None):
+
+    def order(self):
+        return far_first(self.Y) + [0]
+
+    def block(self, d):
+        return self.y_cols(lax.rem(self.y + d + self.Y, self.Y))
+
+    def core_send(self, bufs, d):
+        at = self.block(d)
+        return self.send(bufs[0].at[self.core_half(1 - self.c), at], bufs[1].at[:, at], "c", 1)
+
+    def core_sum(self, bufs, d, copy, w=None):
+        part_sum, got_core, core_sum, got_x = bufs[:4]
+        at, mine = self.block(d), self.core_half(self.c)
+        copy.wait_recv()
+        if w is None:
+            core_sum[:, at] = part_sum[mine, at] + got_core[:, at]
+        else:
+            core_sum[:, at] = part_sum[mine, at] * w[mine, 0:1] + got_core[:, at] * w[mine, 1:2]
+        group = self.group(got_x.at[:, :, at])
+        for e in far_first(self.X):
+            part = self.x_part(lax.rem(self.x + e, self.X))
+            group.send(core_sum.at[part, at], got_x.at[e - 1, :, at], "x", e)
+        return group
+
+    def x_sum(self, bufs, d, from_x, to_y, w=None):
         core_sum, got_x, x_sum, got_y = bufs[2:]
-        total = core_sum[self.x_part(self.x), :]
-        here = self.row_part(self.x)
+        at, here = self.block(d), self.row_part(self.x)
+        from_x.wait_recv()
+        total = core_sum[self.x_part(self.x), at]
         if w is not None:
             total *= w[here, 0:1]
-        for d in range(1, self.X):
-            total += got_x[d - 1] if w is None else got_x[d - 1] * w[here, d : d + 1]
-        x_sum[...] = total
-        return [
-            self.send(x_sum.at[:, self.y_cols(lax.rem(self.y + d, self.Y))], got_y.at[d - 1], "y", d)
-            for d in far_first(self.Y)
-        ]
-
-    def sum_y(self, bufs, w=None):
+        for e in range(1, self.X):
+            total += got_x[e - 1, :, at] if w is None else got_x[e - 1, :, at] * w[here, e : e + 1]
+        x_sum[:, at] = total
+        if d:
+            to_y.send(x_sum.at[:, at], got_y.at[d - 1], "y", d)
+
+    def y_sum(self, bufs, from_y, w=None):
         x_sum, got_y = bufs[4:]
-        total = x_sum[:, self.y_cols(self.y)]
         here = self.row_part(self.x)
+        total = x_sum[:, self.block(0)]
         if w is not None:
             total *= w[here, 0:1]
+        from_y.wait_recv()
         for d in range(1, self.Y):
             total += got_y[d - 1] if w is None else got_y[d - 1] * w[here, d : d + 1]
         return total
 
-    def gather_y(self, dst):
-        own = (self.row_part(self.x), self.y_cols(self.y))
-        return [self.send(dst.at[own], dst.at[own], "y", d) for d in far_first(self.Y)]
-
-    def gather_x(self, pieces):
-        return [(d, [self.send(p, p, "x", d) for p in pieces]) for d in far_first(self.X)]
+    def gather_start(self, dst):
+        own = (self.row_part(self.x), self.block(0))
+        got_y = {d: self.send(dst.at[own], dst.at[own], "y", d) for d in far_first(self.Y)}
+        got_x = {}
+        for e in far_first(self.X):
+            got_x[e] = self.group(dst.at[self.row_part(lax.rem(self.x + self.X - e, self.X))])
+            got_x[e].send(dst.at[own], dst.at[own], "x", e)
+        return got_y, got_x
+
+    def gather_y(self, dst, got_y, got_x, ds):
+        for d in ds:
+            got_y[d].wait_recv()
+            at = (self.row_part(self.x), self.block(-d))
+            for e in far_first(self.X):
+                got_x[e].send(dst.at[at], dst.at[at], "x", e)
 
     def to_core(self, piece):
         return self.send(piece, piece, "c", 1)
 
-    def forward_x(self, got, pieces_of):
+    def gather_x(self, got_x, piece_of):
         out = []
-        for d, copies in got:
-            for cp in copies:
-                cp.wait_recv()
-            xx = lax.rem(self.x + self.X - d, self.X)
-            out += [self.to_core(p) for p in pieces_of(xx)]
+        for e in reversed(far_first(self.X)):
+            got_x[e].wait_recv()
+            out.append(self.to_core(piece_of(lax.rem(self.x + self.X - e, self.X))))
         return out
 
     def __call__(
@@ -177,7 +229,7 @@
         p3, p3c, p3s, p3x, p3t, p3y,
         codes, gcode, gcol, logit, g, acc, st, st_c, st_x, st_y, fin, weights,
         target,
-        local_sem, send_sem, recv_sem,
+        local_sem, send_sem, recv_sem, col_sem,
     ):
         X, Y, C, Z = self.X, self.Y, self.C, self.Z
         rows, rank, vocab = self.rows, self.rank, self.vocab
@@ -205,11 +257,17 @@
         partners = [(a, d) for a, n in zip("xyz", (X, Y, Z)) for d in range(1, n)] + [("c", 1)]
         for a, d in partners:
             pl.semaphore_signal(barrier, inc=1, device_id=self.peer(a, d), device_id_type=MESH)
-        pl.semaphore_wait(barrier, len(partners))
+        for d in range(1, Z):
+            source = (lax.rem(z + d, Z), (self.x * Y + z) * C + c)
+            pl.semaphore_signal(barrier, inc=1, device_id=source, device_id_type=MESH)
+        sends_cols = (lax.rem(z - self.y + Z, Z) + Z - 1) // Z
+        pl.semaphore_wait(barrier, len(partners) + Y * sends_cols)
 
         for cp in loads:
             cp.wait()
-        downs = [self.send(down_slot, down_slot, "z", d) for d in far_first(Z)]
+        downs = self.group(dn.at[:, pl.ds(0, (Z - 1) * self.code_col)])
+        for d in far_first(Z):
+            downs.send(down_slot, down_slot, "z", d)
         acc[...] = jnp.zeros_like(acc)
         meta[0] = jnp.zeros((8, rows), F32)
         some, lanes = rows // 4, rows // 2
@@ -232,63 +290,68 @@
             return 0
 
         lax.fori_loop(0, rank // WIDE, target_tile, 0)
-        mine3, theirs3 = self.core_half(c), self.core_half(1 - c)
+        mine, theirs = self.core_half(c), self.core_half(1 - c)
         b1 = (p1, p1c, p1s, p1x, p1t, p1y)
         b2 = (p2, p2c, p2s, p2x, p2t, p2y)
         b3 = (p3, p3c, p3s, p3x, p3t, p3y)
-        core3 = self.send(p3.at[theirs3], p3c, "c", 1)
-        for cp in downs:
-            cp.wait_recv()
-        p1[theirs3, :] = jnp.dot(hid[0, theirs3], dn[...], preferred_element_type=F32)
-        core1 = self.send(p1.at[theirs3], p1c, "c", 1)
-        p1[mine3, :] = jnp.dot(hid[0, mine3], dn[...], preferred_element_type=F32)
-        others = [self.send(hid.at[0], hid.at[Z - d], "z", d) for d in far_first(Z)]
-        metas = [self.send(meta.at[0], meta.at[Z - d], "z", d) for d in far_first(Z)]
-        core1.wait_recv()
-        got1 = self.sum_core(b1)
+        order = self.order()
+        core3 = self.send(p3.at[theirs], p3c, "c", 1)
+        downs.wait_recv()
+        p1[theirs, :] = jnp.dot(hid[0, theirs], dn[...], preferred_element_type=F32)
+        core1 = {d: self.core_send(b1, d) for d in order}
+        p1[mine, :] = jnp.dot(hid[0, mine], dn[...], preferred_element_type=F32)
+        x1 = {d: self.core_sum(b1, d, core1[d]) for d in order}
+        others = self.group(hid.at[pl.ds(1, Z - 1)])
+        metas = self.group(meta.at[pl.ds(1, Z - 1)])
+        for d in far_first(Z):
+            others.send(hid.at[0], hid.at[Z - d], "z", d)
+            metas.send(meta.at[0], meta.at[Z - d], "z", d)
+        y1 = self.group(p1y)
+        for d in order:
+            self.x_sum(b1, d, x1[d], y1)
         core3.wait_recv()
-        for cp in got1:
-            cp.wait_recv()
-        got1 = self.sum_x(b1)
-        got3 = self.sum_core(b3)
-        for cp in got1:
-            cp.wait_recv()
-        block = self.sum_y(b1)
+        p3s[...] = p3[mine, :] + p3c[...]
+        x3 = self.group(p3x)
+        for e in far_first(X):
+            x3.send(p3s.at[self.x_part(lax.rem(self.x + e, X))], p3x.at[e - 1], "x", e)
+        block = self.y_sum(b1, y1)
         own = codes.at[0]
-        own[self.row_part(self.x), self.y_cols(self.y)] = block.astype(BF16)
-        for cp in self.gather_y(own):
-            cp.wait_recv()
-        got = self.gather_x([own.at[self.row_part(self.x)]])
+        own[self.row_part(self.x), self.block(0)] = block.astype(BF16)
+        got_y, got_x = self.gather_start(own)
+        near_first = list(reversed(far_first(Y)))
+        self.gather_y(own, got_y, got_x, near_first)
         cores = [self.to_core(own.at[self.row_part(self.x)])]
-        cores += self.forward_x(got, lambda xx: [own.at[self.row_part(xx)]])
-
-        ring = {}
+        cores += self.gather_x(got_x, lambda xx: own.at[self.row_part(xx)])
 
         def quarter(right):
             n = self.half // 2
             return pl.ds(pl.multiple_of(c * self.half + (0 if right else n), n), n)
 
+        def ring_copy(s, right):
+            src = (Z - (s - 1)) % Z if right else s - 1
+            dst = Z - s if right else s
+            part = quarter(right) if s == Z // 2 else self.core_half(c)
+            return self.make(codes.at[src, part], codes.at[dst, part], "z", 1 if right else Z - 1)
+
+        ring = {s: [ring_copy(s, True), ring_copy(s, False)] for s in range(1, Z // 2 + 1)}
+        handed = {
+            s: self.make(codes.at[s, self.core_half(c)], codes.at[s, self.core_half(c)], "c", 1)
+            for s in range(1, Z)
+        }
+
         def ring_send(s):
-            last = s == Z // 2
-            copies = []
-            for right in (True, False):
-                src = (Z - (s - 1)) % Z if right else s - 1
-                dst = Z - s if right else s
-                part = quarter(right) if last else self.core_half(c)
-                copies.append(self.send(codes.at[src, part], codes.at[dst, part], "z", 1 if right else Z - 1))
-            ring[s] = copies
-
-        handed = {}
+            for cp in ring[s]:
+                cp.start()
 
         def ring_step(s):
+            if s > Z // 2:
+                return
             for cp in ring[s]:
                 cp.wait_recv()
             if s < Z // 2:
                 ring_send(s + 1)
-                for slot in (Z - s, s):
-                    handed[slot] = self.to_core(codes.at[slot, self.core_half(c)])
-            else:
-                handed[s] = self.to_core(codes.at[s, self.core_half(c)])
+                handed[Z - s].start()
+            handed[s].start()
 
         ring_send(1)
         for cp in cores:
@@ -341,9 +404,12 @@
             columns(k, w)
             return top, sum(s[1] * f for s, f in zip(stats, w)), sum(s[2] for s in stats)
 
-        def swap(k, axis, n, got):
-            put(st.at[k], *mine)
-            return [self.send(st.at[k], got(d), axis, d) for d in far_first(n)]
+        def swap(k, axis, n, total, got):
+            put(st.at[k], *mine_st)
+            group = self.group(total)
+            for d in far_first(n):
+                group.send(st.at[k], got(d), axis, d)
+            return group
 
         def got_all(copies):
             for cp in copies:
@@ -351,19 +417,23 @@
 
         st[...] = jnp.zeros_like(st)
         fin[0] = jnp.zeros((8, rows), F32)
-        mine = (peak, total, picked)
-        stats = swap(0, "c", C, lambda d: st_c)
-        core2 = []
-        for i in range(rank // WIDE):
-            at = pl.ds(i * WIDE, WIDE)
-            p2[:, at] = jnp.dot(g[...], u[:, at], preferred_element_type=F32)
-            core2.append(self.send(p2.at[theirs3, at], p2c.at[:, at], "c", 1))
-        got_all(stats)
-        mine = merge(0, [mine, take(st_c)])
-        stats = swap(1, "x", X, lambda d: st_x.at[d - 1])
+        mine_st = (peak, total, picked)
+        stats = swap(0, "c", C, st_c, lambda d: st_c)
+        core2, x2 = {}, {}
+        for i in range(Y + 2):
+            if i < Y:
+                at = self.block(order[i])
+                p2[:, at] = jnp.dot(g[...], u[:, at], preferred_element_type=F32)
+                core2[order[i]] = self.core_send(b2, order[i])
+            if i == 1:
+                stats.wait_recv()
+                mine_st = merge(0, [mine_st, take(st_c)])
+                stats = swap(1, "x", X, st_x, lambda d: st_x.at[d - 1])
+            if i >= 2:
+                d = order[i - 2]
+                x2[d] = self.core_sum(b2, d, core2[d], weights.at[0])
 
         def logits_of(slot):
-            handed[slot].wait_recv()
             lax.fori_loop(0, tiles, lambda i, _: (logit_tile(slot, i), 0)[1], 0)
 
         def gradient_of(slot):
@@ -380,79 +450,149 @@
 
             lax.fori_loop(0, tiles, tile, 0)
 
-        got_all(core2)
-        got2 = self.sum_core(b2, weights.at[0], weights.at[0])
-        got_all(got3)
-        got3 = self.sum_x(b3)
+        early = min(2, Z - 1)
+
+        def plane(o):
+            return (1 - o % 2) * (o // 2) + (o % 2) * (Z - (o + 1) // 2)
+
+        x3.wait_recv()
+        p3t[...] = functools.reduce(
+            jnp.add, [p3x[e - 1] for e in range(1, X)], p3s[self.x_part(self.x), :]
+        )
+        y3 = self.group(p3y)
+        for d in far_first(Y):
+            y3.send(p3t.at[:, self.block(d)], p3y.at[d - 1], "y", d)
         ring_step(1)
-        got_all(stats)
-        mine = merge(1, [mine] + [take(st_x.at[d - 1]) for d in range(1, X)])
-        stats = swap(2, "y", Y, lambda d: st_y.at[d - 1])
-        planes = [s for d in range(1, Z // 2) for s in (Z - d, d)] + [Z // 2]
-        early = planes[:4] if Z > 4 else planes[:1]
-        late = [s for s in planes if s not in early]
-        for s in early[:2]:
-            logits_of(s)
-        got_all(got2)
-        got2 = self.sum_x(b2, weights.at[1])
-        got_all(stats)
-        top, total, picked = merge(2, [mine] + [take(st_y.at[d - 1]) for d in range(1, Y)])
+        stats.wait_recv()
+        mine_st = merge(1, [mine_st] + [take(st_x.at[d - 1]) for d in range(1, X)])
+        stats = swap(2, "y", Y, st_y, lambda d: st_y.at[d - 1])
+        for o in range(1, early + 1):
+            handed[plane(o)].wait_recv()
+        lax.fori_loop(1, early + 1, lambda o, _: (logits_of(plane(o)), 0)[1], 0)
+        y2 = self.group(p2y)
+        for d in order:
+            self.x_sum(b2, d, x2[d], y2, weights.at[1])
+        stats.wait_recv()
+        top, total, picked = merge(2, [mine_st] + [take(st_y.at[d - 1]) for d in range(1, Y)])
         weight = scale / total
         put(fin.at[0], top, weight, picked)
-        finals = [self.send(fin.at[0], fin.at[Z - d], "z", d) for d in far_first(Z)]
+        finals = self.group(fin.at[pl.ds(1, Z - 1)])
+        for d in far_first(Z):
+            finals.send(fin.at[0], fin.at[Z - d], "z", d)
         hit_grad = (scale * (jnp.exp(picked - top) / total - 1.0)).astype(BF16).astype(F32)
         columns(3, [weight, hit_grad])
+        ring_step(2)
+        target_row = self.y_sum(b3, y3)
+        here = self.row_part(self.x)
+        block = self.y_sum(b2, y2, weights.at[2]) * weights[3, here, 0:1]
+        block += weights[3, here, 1:2] * target_row.astype(F32)
+        gcode[here, self.block(0)] = block.astype(BF16)
+        got_y, got_x = self.gather_start(gcode)
+
+        def pieces(ref, axis, e):
+            return self.make(ref, ref, axis, e)
+
+        passed = {}
+        for d in near_first:
+            ref = gcode.at[here, self.block(-d)]
+            passed[d] = [got_x[e].add(ref, ref, "x", e).copies[-1] for e in far_first(X)]
+
+        def other(e):
+            return self.row_part(lax.rem(self.x + X - e, X))
+
+        near_x = list(reversed(far_first(X)))
+        to_core = pieces(gcode.at[here], "c", 1)
+        from_x = {e: pieces(gcode.at[other(e)], "c", 1) for e in near_x}
+        rest = pl.ds(1, Z - 1)
+        cols_x = {e: pieces(gcol.at[rest, here], "x", e) for e in far_first(X)}
+        cols_core = pieces(gcol.at[rest, here], "c", 1)
+        cols_from_x = {e: pieces(gcol.at[rest, other(e)], "c", 1) for e in near_x}
+        slot = lax.rem(z + Z - self.y, Z)
+
+        def col_copy(k, src, dst):
+            return pltpu.make_async_remote_copy(
+                src_ref=src,
+                dst_ref=dst,
+                send_sem=col_sem.at[0],
+                recv_sem=col_sem.at[1],
+                device_id=(self.y, (self.x * Y + lax.rem(self.y + k, Y)) * C + c),
+                device_id_type=MESH,
+            )
+
+        @pl.when(z != self.y)
+        def _():
+            for k in [0] + far_first(Y):
+                col_copy(k, gcode.at[here, self.block(0)], gcol.at[slot, here]).start()
+
         loss = top + jnp.log(total) - picked
         for i in range(2):
             pair = jnp.broadcast_to(loss[:, i * lanes : (i + 1) * lanes], (8, lanes))
             loss_out[2 * i : 2 * i + 1, :] = pair[0:1, :some]
             loss_out[2 * i + 1 : 2 * i + 2, :] = pltpu.roll(pair, some, axis=1)[0:1, :some]
-        if Z > 2:
-            ring_step(2)
-        for s in early[2:]:
-            logits_of(s)
-        got_all(got3)
-        target_row = self.sum_y(b3)
-        got_all(got2)
-        here = self.row_part(self.x)
-        block = self.sum_y(b2, weights.at[2]) * weights[3, here, 0:1]
-        block += weights[3, here, 1:2] * target_row.astype(F32)
-        gcode[here, self.y_cols(self.y)] = block.astype(BF16)
-        got = self.gather_y(gcode)
-        gradient_of(0)
-        if Z > 4:
-            ring_step(3)
-        got_all(finals + metas + others)
-        gradient_of(early[0])
-        got_all(got)
-        got = self.gather_x([gcode.at[here]])
-        cols = [
-            self.send(
-                gcode.at[here, self.z_cols(lax.rem(z + d, Z))], gcol.at[Z - d, here], "z", d
-            )
-            for d in far_first(Z)
-        ]
-        cores = [self.to_core(gcode.at[here])]
-        for s in early[1:3]:
-            gradient_of(s)
-        got_all(cols)
-        got_cols = self.gather_x([gcol.at[pl.ds(1, Z - 1), here]])
-        col_cores = [self.to_core(gcol.at[pl.ds(1, Z - 1), here])]
-        cores += self.forward_x(got, lambda xx: [gcode.at[self.row_part(xx)]])
-        if Z > 6:
-            ring_step(4)
-        for s in early[3:]:
-            gradient_of(s)
-        for s in late[:1]:
-            logits_of(s)
-            gradient_of(s)
-        col_cores += self.forward_x(got_cols, lambda xx: [gcol.at[pl.ds(1, Z - 1), self.row_part(xx)]])
+        def pass_y(ds):
+            for d in ds:
+                got_y[d].wait_recv()
+                for cp in passed[d]:
+                    cp.start()
+
+        def pass_cols():
+            got = gcol.at[pl.ds(1, Z - 1), here]
+            col_copy(0, got, got).wait_recv()
+            for e in far_first(X):
+                cols_x[e].start()
+            cols_core.start()
+
+        def pass_x():
+            for e in near_x:
+                got_x[e].wait_recv()
+                from_x[e].start()
+
+        def pass_cols_x():
+            for e in near_x:
+                cols_x[e].wait_recv()
+                cols_from_x[e].start()
+
+        events = {}
+
+        def at_step(o, place, *todo):
+            events.setdefault((min(o, Z - 1), place), []).extend(todo)
+
+        at_step(1, 0, lambda: pass_y(near_first[: Y // 2]), lambda: got_all([finals, metas, others]))
+        at_step(2, 0, lambda: pass_y(near_first[Y // 2 :]), to_core.start)
+        at_step(3, 1, lambda: ring_step(3))
+        at_step(4, 0, pass_x, pass_cols)
+        at_step(5, 1, lambda: ring_step(4))
+        at_step(6, 0, pass_cols_x)
+        for o in range(early + 1, Z):
+            at_step(o, 0, handed[plane(o)].wait_recv)
+
+        def run(o, place):
+            for k in range(Z):
+                if (k, place) in events:
+
+                    @pl.when(o == k)
+                    def _():
+                        for todo in events[k, place]:
+                            todo()
+
+        def step(o, _):
+            slot = plane(o)
+            run(o, 0)
+
+            @pl.when(o > early)
+            def _():
+                logits_of(slot)
+
+            run(o, 1)
+            gradient_of(slot)
+            return 0
+
+        lax.fori_loop(0, Z, step, 0)
+        cores = [to_core, *from_x.values()]
+        col_cores = [cols_core, *cols_from_x.values()]
         got_all(cores)
         gh_out[...] = lax.dot_general(gcode[...], dn[...], NT, preferred_element_type=F32)
         gcol[0] = gcode[:, self.z_cols(z)]
-        for s in late[1:]:
-            logits_of(s)
-            gradient_of(s)
         gu_out[...] = acc[...].astype(BF16)
         got_all(col_cores)
         gd_out[...] = lax.dot_general(
@@ -463,6 +603,13 @@
         )
         for cp in self.sent:
             cp.wait_send()
+        if self.sems > SEMS:
+            raise ValueError(self.sems)
+
+        @pl.when(z != self.y)
+        def _():
+            gone = gcol.at[:, here]
+            col_copy(0, gone, gone).wait_send()
 
 
 def hand_over(*refs):

time: 90.1 us -> 86.1 us (0.956)
  Pallas kernels: 89.3 us -> 85.3 us
    pallas_call x1, Pallas kernels: 88.4 us -> 84.4 us  [shards(): pl.pallas_call(kernel.__call__, out_shape=tuple((pltpu.VMEM(s.shape, s.dt...]
where the time goes in v3:
time: 86.1 us; the launch traced here: 86 us
  Pallas kernels  85.3 us (99%)
    pallas_call x1, Pallas kernels, shards(): pl.pallas_call(kernel.__call__, out_shape=tuple((pltpu.VMEM(s.shape, s.dt...  84.4 us

profile of v3, /device:TPU:1, one launch (start us, length us, event | category | flops | bytes accessed | tf_op | source)
XLA Modules:
  0.0 86.0 jit_solution(14628209551711837399)
XLA Ops:
  0.6 84.4 %fused.1 = (f32[4,64]{1,0:T(4,128)S(1)}, f32[256,112]{1,0:T(8,128)S(1)}, f32[112,128]{1,0:T(8,128)S(1)}, bf16[2048,128]{1,0:T(8,128)(2,1)S(1)}) custom-call(bf16[2048,1024]{1,0:T(8,128)(2,1)} %u_hbm.1, bf16[256,112]{1,0:T(8,128)(2,1)} %bitcast.2, bf16[112,128]{1,0:T(8,128)(2,1)} %down_hbm.1, s32[4,64]{1,0:T(4,128)} %target_hbm.1, f32[4]{0:T(128)} %scale_ref.1), custom_call_target="tpu_custom_call" | custom-call | tf_op jit(solution)/shard_map/fused/pallas_call | solution.py:638
  85.1 0.9 %results.1 = (f32[4,64]{1,0:T(4,128)}, f32[256,112]{1,0:T(8,128)}, f32[112,128]{1,0:T(8,128)}, bf16[2048,128]{1,0:T(8,128)(2,1)}) custom-call(f32[4,64]{1,0:T(4,128)S(1)} %get-tuple-element.12.refs_0_, f32[256,112]{1,0:T(8,128)S(1)} %get-tuple-element.13.refs_1_, f32[112,128]{1,0:T(8,128)S(1)} %get-tuple-element.14.refs_2_, ...), custom_call_target="tpu_custom_call" | custom-call | tf_op jit(solution)/shard_map/results/pallas_call | solution.py:649
